TPU v7x, 32 devices: a whole 2x2x4 slice. The times are simulated.
32 devices in a mesh: gx: 4 (over z), gy: 2 (over y), af: 4 (over x, core).
Axes of the slice: x: 2, y: 2, z: 4, core: 2. Of those that a mesh axis runs over, the one named last changes fastest.
Arguments:
- electric: float32 [3, 64, 16, 512], P(None, 'gx', 'gy', 'af'), may hold values from -6 to 6
- material: int32 [64, 16, 512], P('gx', 'gy', 'af'), may hold values from 0 to 15
- coef_keep: float32 [3, 16], replicated, may hold values from 0.6 to 1
- coef_curl: float32 [3, 16], replicated, may hold values from 0.1 to 0.5
- huygens_count: int32 [4, 2, 4], P('gx', 'gy', 'af'), may hold values from 1 to 512, as said below
- huygens_cells: int32 [4, 2, 4, 512], P('gx', 'gy', 'af'), may hold values from 0 to 16383
- band_tiles: int32 [8, 8, 4], P(('gx', 'gy'), 'af'), may hold values from 0 to 15, as said below
- radiation: bfloat16 [8, 8, 4, 6, 128, 128], P('af', ('gx', 'gy')), may hold values from -0.0390625 to 0.0390625
Outputs:
- electric_end: float32 [3, 64, 16, 512], P(None, 'gx', 'gy', 'af')
- magnetic_end: float32 [3, 64, 16, 512], P(None, 'gx', 'gy', 'af')
- pattern: float32 [4, 1024], P(None, 'af')
Inputs may be any that keep to these rules, and one draw needn't show every extreme that they name: `huygens_count`: every brick has 1 to 512 live rows, and some brick has exactly 512. `band_tiles`: the 4 tiles of one group and direction block are distinct, and every tile of a group is listed by some direction block.
All inputs are finite; a program needn't handle non-finite values.
Results may differ from a plain program's by a relative error of at most 0.0029.
Values may be sent and summed in bfloat16 or wider, within the bound.
A program may use at most 64 MiB of HBM per device.

v0:
```python
import functools

import jax
import jax.numpy as jnp
from jax import lax
from jax.experimental import pallas as pl
from jax.experimental.pallas import tpu as pltpu
from jax.sharding import PartitionSpec as P

STEPS = 4
COURANT = 0.5
MESH = pl.DeviceIdType.MESH

XLO_Y, XLO_Z = 0, 1
XHI_X, XHI_Y, XHI_Z = 2, 3, 4
YLO_Z, YLO_X = 5, 7
YHI_X, YHI_Y, YHI_Z = 9, 11, 13
ZLO_X, ZLO_Y = 15, 16
ZHI_X, ZHI_Y, ZHI_Z = 17, 18, 19
FACES = 20
EDGE_XZ, EDGE_XY, EDGE_YZ, EDGE_YX, EDGE_ZY, EDGE_ZX = 20, 21, 22, 24, 25, 26
GHOSTS = 27

MESSAGES = (
    (ZLO_X, 1, EDGE_XZ, (1, 0, -1)),
    (XHI_X, 1, EDGE_XY, (1, -1, 0)),
    (YHI_Y, 2, EDGE_YZ, (0, 1, -1)),
    (XLO_Y, 1, EDGE_YX, (-1, 1, 0)),
    (ZHI_Z, 1, EDGE_ZY, (0, -1, 1)),
    (ZHI_Z, 1, EDGE_ZX, (-1, 0, 1)),
    (YHI_X, 6, YHI_X, (0, 1, 0)),
    (YLO_Z, 4, YLO_Z, (0, -1, 0)),
    (ZLO_X, 2, ZLO_X, (0, 0, -1)),
    (ZHI_X, 3, ZHI_X, (0, 0, 1)),
    (XLO_Y, 2, XLO_Y, (-1, 0, 0)),
    (XHI_X, 3, XHI_X, (1, 0, 0)),
)


def kernel(
    sizes,
    electric_in, material_in, keep_in, curl_in, count_in, cells_in, band_in, radiation,
    e_end, h_end, p_end,
    e_out, h_out, pattern, material, coef_keep, coef_curl, count, cells, band, face, ghost, hgx, hgy, hgz, keep, gain, table, zhot, rhot, rows, weights, shares,
    send_sem, recv_sem, row_send, row_recv, share_send, share_recv, load_sem, store_sem,
):
    n_gx, n_gy, n_af = sizes
    groups = n_gx * n_gy
    gx, gy, af = lax.axis_index("gx"), lax.axis_index("gy"), lax.axis_index("af")
    me = (gx, gy, af)
    group = gx * n_gy + gy
    cx, cy, cz = e_out.shape[1:]
    hmax = cells.shape[-1]
    row_tile = radiation.shape[-1]
    tiles = hmax // row_tile
    owned, entries, comps = radiation.shape[0], radiation.shape[2], radiation.shape[3]

    def exists(step):
        ok = None
        for at, d, n in zip(me, step, sizes):
            if d:
                term = (at + d >= 0) if d < 0 else (at + d < n)
                ok = term if ok is None else jnp.logical_and(ok, term)
        return ok

    def place(step):
        return tuple(jnp.clip(at + d, 0, n - 1) if d else at for at, d, n in zip(me, step, sizes))

    def back(step):
        return tuple(-d for d in step)

    def af_peer(off):
        return (gx, gy, lax.rem(af + off, n_af))

    def group_peer(off):
        other = lax.rem(group + off, groups)
        return (other // n_gy, lax.rem(other, n_gy), af)

    def over_groups(body):
        if groups <= 16:
            for off in range(1, groups):
                body(off)
        else:
            def step(off, carry):
                body(off)
                return carry
            lax.fori_loop(1, groups, step, 0)

    loads = [
        pltpu.make_async_copy(src, dst, load_sem.at[i])
        for i, (src, dst) in enumerate((
            (electric_in, e_out), (material_in, material), (keep_in, coef_keep),
            (curl_in, coef_curl), (cells_in, cells), (count_in, count), (band_in, band),
            (radiation, weights),
        ))
    ]
    for load in loads:
        load.start()
    stores = [
        pltpu.make_async_copy(src, dst, store_sem.at[i])
        for i, (src, dst) in enumerate(((e_out, e_end), (h_out, h_end), (pattern, p_end)))
    ]

    barrier = pltpu.get_barrier_semaphore()
    for off in range(1, n_af):
        pl.semaphore_signal(barrier, inc=1, device_id=af_peer(off), device_id_type=MESH)
    over_groups(lambda off: pl.semaphore_signal(
        barrier, inc=1, device_id=group_peer(off), device_id_type=MESH))
    expected = jnp.int32(n_af - 1 + groups - 1)
    for _, _, _, step in MESSAGES:
        if step[2] and (step[0] or step[1]):
            there = exists(step)
            expected = expected + there.astype(jnp.int32)

            @pl.when(there)
            def _(step=step):
                pl.semaphore_signal(barrier, inc=1, device_id=place(step), device_id_type=MESH)

    lane = lax.broadcasted_iota(jnp.int32, (cy, cz), 1)
    sub = lax.broadcasted_iota(jnp.int32, (cy, cz), 0)
    lane2 = lax.broadcasted_iota(jnp.int32, (cx, cz), 1)
    sub2 = lax.broadcasted_iota(jnp.int32, (cx, cz), 0)

    def up_z(v, col):
        n = v.shape[0]
        return jnp.where((lane if n == cy else lane2) == cz - 1, col, pltpu.roll(v, cz - 1, 1))

    def up_s(v, row):
        n = v.shape[0]
        return jnp.where((sub if n == cy else sub2) == n - 1, row, pltpu.roll(v, n - 1, 0))

    def pack_plane(t, i, ex, ey, ez, packed):
        face[t, YLO_Z + i // 8, i % 8 : i % 8 + 1, :] = ez[0:1]
        face[t, YLO_X + i // 8, i % 8 : i % 8 + 1, :] = ex[0:1]
        face[t, YHI_X + i // 8, i % 8 : i % 8 + 1, :] = ex[cy - 1 : cy]
        face[t, YHI_Y + i // 8, i % 8 : i % 8 + 1, :] = ey[cy - 1 : cy]
        face[t, YHI_Z + i // 8, i % 8 : i % 8 + 1, :] = ez[cy - 1 : cy]
        if i == 0:
            face[t, XLO_Y] = ey
            face[t, XLO_Z] = ez
        if i == cx - 1:
            face[t, XHI_X] = ex
            face[t, XHI_Y] = ey
            face[t, XHI_Z] = ez
        cols = (ex[:, 0:1], ey[:, 0:1], ex[:, cz - 1 :], ey[:, cz - 1 :], ez[:, cz - 1 :])
        packed = [jnp.where(lane == i, col, p) for col, p in zip(cols, packed)]
        if i == cx - 1:
            for slot, p in zip((ZLO_X, ZLO_Y, ZHI_X, ZHI_Y, ZHI_Z), packed):
                face[t, slot] = p
        return packed

    loads[0].wait()
    nothing = [jnp.zeros((cy, cz), jnp.float32)] * 5
    packed = nothing
    for i in range(cx):
        packed = pack_plane(0, i, e_out[0, i], e_out[1, i], e_out[2, i], packed)

    for m, (_, n, at, step) in enumerate(MESSAGES):
        @pl.when(jnp.logical_not(exists(back(step))))
        def _(n=n, at=at):
            for t in range(STEPS):
                for r in range(at, at + n):
                    ghost[t, r] = jnp.zeros((cy, cz), jnp.float32)

    def message(t, m):
        first, n, at, step = MESSAGES[m]
        return pltpu.make_async_remote_copy(
            src_ref=face.at[t, pl.ds(first, n)],
            dst_ref=ghost.at[t, pl.ds(at, n)],
            send_sem=send_sem.at[t, m],
            recv_sem=recv_sem.at[t, m],
            device_id=place(step),
            device_id_type=MESH,
        )

    def send_faces(t):
        for m in range(len(MESSAGES)):
            @pl.when(exists(MESSAGES[m][3]))
            def _(m=m):
                message(t, m).start()

    def receive_faces(t):
        for m in range(len(MESSAGES)):
            @pl.when(exists(back(MESSAGES[m][3])))
            def _(m=m):
                message(t, m).wait_recv()

    pl.semaphore_wait(barrier, expected)
    send_faces(0)

    for load in loads[1:-1]:
        load.wait()
    table[...] = jnp.zeros_like(table)
    mats = coef_keep.shape[1]
    table[0:3, 0:mats] = coef_keep[...]
    table[3:6, 0:mats] = coef_curl[...]
    for c in range(6):
        row = jnp.broadcast_to(table[c : c + 1, :], (cy, cz))
        for i in range(cx):
            picked = jnp.take_along_axis(row, material[i], axis=1, mode="promise_in_bounds")
            if c < 3:
                keep[c, i] = picked
            else:
                gain[c - 3, i] = picked
    cell = jnp.broadcast_to(cells[...].reshape(1, hmax), (cz, hmax))
    zhot[...] = (lax.broadcasted_iota(jnp.int32, (cz, hmax), 0) == lax.rem(cell, cz)).astype(
        jnp.float32).astype(jnp.bfloat16)
    cell = jnp.broadcast_to(cells[...].reshape(1, hmax), (cx * cy, hmax))
    live = lax.broadcasted_iota(jnp.int32, (cx * cy, hmax), 1) < count[0, 0, 0]
    rhot[...] = jnp.logical_and(
        lax.broadcasted_iota(jnp.int32, (cx * cy, hmax), 0) == lax.div(cell, cz), live
    ).astype(jnp.float32)

    has_x = (gx > 0).astype(jnp.float32)
    has_y = (gy > 0).astype(jnp.float32)
    has_z = (af > 0).astype(jnp.float32)

    def row_message(t, off):
        mine = rows.at[t, pl.ds(af * (tiles // 2), tiles // 2)]
        return pltpu.make_async_remote_copy(
            src_ref=mine, dst_ref=mine,
            send_sem=row_send.at[t, off], recv_sem=row_recv.at[t, off],
            device_id=af_peer(off), device_id_type=MESH,
        )

    for t in range(STEPS):
        receive_faces(t)

        def two(r):
            return ghost[t, r : r + 2].reshape(cx, cz)

        def grown(old, ref, at, change, there):
            new = -COURANT * change * there
            if t:
                new = old + new
            ref[at] = new

        ex, ey, ez = ghost[t, XHI_X], ghost[t, XHI_Y], ghost[t, XHI_Z]
        dz_ex = up_z(ex, ghost[t, EDGE_XZ][:, cx - 1 : cx]) - ex
        dy_ex = up_s(ex, ghost[t, EDGE_XY, 0:1, :]) - ex
        grown(hgx[0], hgx, 0, dz_ex - (e_out[2, 0] - ez), has_x)
        grown(hgx[1], hgx, 1, (e_out[1, 0] - ey) - dy_ex, has_x)

        ex, ey, ez = two(YHI_X), two(YHI_Y), two(YHI_Z)
        low_z = face[t, YLO_Z : YLO_Z + 2].reshape(cx, cz)
        low_x = face[t, YLO_X : YLO_X + 2].reshape(cx, cz)
        dz_ey = up_z(ey, two(EDGE_YZ)[:, 0:1]) - ey
        dx_ey = up_s(ey, ghost[t, EDGE_YX, cy - 1 : cy, :]) - ey
        grown(hgy[0], hgy, 0, (low_z - ez) - dz_ey, has_y)
        grown(hgy[1], hgy, 1, dx_ey - (low_x - ex), has_y)

        ex, ey, ez = ghost[t, ZHI_X], ghost[t, ZHI_Y], ghost[t, ZHI_Z]
        dy_ez = up_s(ez, ghost[t, EDGE_ZY, 0:1, :]) - ez
        dx_ez = jnp.where(
            lane == cx - 1, ghost[t, EDGE_ZX][:, 0:1], pltpu.roll(ez, cz - 1, 1)) - ez
        grown(hgz[0], hgz, 0, dy_ez - (face[t, ZLO_Y] - ey), has_z)
        grown(hgz[1], hgz, 1, (face[t, ZLO_X] - ex) - dx_ez, has_z)

        top_x, top_y = ghost[t, ZLO_X], ghost[t, ZLO_Y]
        low_hx, low_hy = hgz[0], hgz[1]
        hy_last, hz_last = hgx[0], hgx[1]
        packed = nothing
        ex, ey, ez = e_out[0, 0], e_out[1, 0], e_out[2, 0]
        for i in range(cx):
            if i + 1 < cx:
                exn, eyn, ezn = e_out[0, i + 1], e_out[1, i + 1], e_out[2, i + 1]
            else:
                exn, eyn, ezn = None, ghost[t, XLO_Y], ghost[t, XLO_Z]
            up = (i // 8, slice(i % 8, i % 8 + 1))
            ez_y = up_s(ez, ghost[t, YLO_Z + up[0], up[1], :])
            ex_y = up_s(ex, ghost[t, YLO_X + up[0], up[1], :])
            ex_z = up_z(ex, top_x[:, i : i + 1])
            ey_z = up_z(ey, top_y[:, i : i + 1])
            hx = -COURANT * ((ez_y - ez) - (ey_z - ey))
            hy = -COURANT * ((ex_z - ex) - (ezn - ez))
            hz = -COURANT * ((eyn - ey) - (ex_y - ex))
            if t:
                hx = h_out[0, i] + hx
                hy = h_out[1, i] + hy
                hz = h_out[2, i] + hz
            h_out[0, i], h_out[1, i], h_out[2, i] = hx, hy, hz
            hx_y = jnp.where(sub == 0, hgy[0, i : i + 1, :], pltpu.roll(hx, 1, 0))
            hz_y = jnp.where(sub == 0, hgy[1, i : i + 1, :], pltpu.roll(hz, 1, 0))
            hx_z = jnp.where(lane == 0, low_hx[:, i : i + 1], pltpu.roll(hx, 1, 1))
            hy_z = jnp.where(lane == 0, low_hy[:, i : i + 1], pltpu.roll(hy, 1, 1))
            curl_x = (hz - hz_y) - (hy - hy_z)
            curl_y = (hx - hx_z) - (hz - hz_last)
            curl_z = (hy - hy_last) - (hx - hx_y)
            hy_last, hz_last = hy, hz
            new_x = keep[0, i] * ex + gain[0, i] * curl_x
            new_y = keep[1, i] * ey + gain[1, i] * curl_y
            new_z = keep[2, i] * ez + gain[2, i] * curl_z
            e_out[0, i], e_out[1, i], e_out[2, i] = new_x, new_y, new_z
            if t + 1 < STEPS:
                packed = pack_plane(t + 1, i, new_x, new_y, new_z, packed)
            ex, ey, ez = exn, eyn, ezn
        if t + 1 < STEPS:
            send_faces(t + 1)
        else:
            stores[0].start()
            stores[1].start()

        picked = []
        for k in range(comps):
            field = e_out if k < 3 else h_out
            values = field[k % 3].reshape(cx * cy, cz).astype(jnp.bfloat16)
            column = jnp.dot(values, zhot[...], preferred_element_type=jnp.float32)
            picked.append(jnp.sum(column * rhot[...], axis=0, keepdims=True))
        picked.append(jnp.zeros((8 - comps, hmax), jnp.float32))
        picked = jnp.concatenate(picked, axis=0)
        for q in range(tiles // 2):
            at = 2 * q * row_tile
            pair = [picked[:, at : at + row_tile], picked[:, at + row_tile : at + 2 * row_tile]]
            rows[t, af * (tiles // 2) + q] = jnp.concatenate(pair, axis=0).astype(jnp.bfloat16)
        for off in range(1, n_af):
            row_message(t, off).start()

    loads[-1].wait()
    for t in range(STEPS):
        for off in range(1, n_af):
            row_message(t, off).wait_recv()

    sums = []
    for o in range(owned):
        total = None
        for n in range(entries):
            tile = band[0, o, n]
            pairs = [rows[t, tile // 2].astype(jnp.float32) for t in range(STEPS)]
            odd = lax.rem(tile, 2)
            segment = jnp.concatenate(
                [jnp.where(odd == 1, pair[8:], pair[:8]) for pair in pairs], axis=0)
            term = lax.dot_general(
                segment.astype(jnp.bfloat16),
                weights[o, 0, n].reshape(comps * row_tile, row_tile),
                (((1,), (1,)), ((), ())),
                preferred_element_type=jnp.float32,
            )
            total = term if total is None else total + term
        for t in range(STEPS):
            own = total[t * 8 : t * 8 + 1, 0:row_tile]
            for k in range(1, comps):
                own = own + total[t * 8 + k : t * 8 + k + 1, k * row_tile : (k + 1) * row_tile]
            sums.append(own)
    shares[group] = jnp.concatenate(sums, axis=0)

    def share_message(off):
        return pltpu.make_async_remote_copy(
            src_ref=shares.at[group], dst_ref=shares.at[group],
            send_sem=share_send.at[off], recv_sem=share_recv.at[off],
            device_id=group_peer(off), device_id_type=MESH,
        )

    over_groups(lambda off: share_message(off).start())
    for t in range(STEPS):
        for off in range(1, n_af):
            row_message(t, off).wait_send()
        for m in range(len(MESSAGES)):
            @pl.when(exists(MESSAGES[m][3]))
            def _(t=t, m=m):
                message(t, m).wait_send()
    stores[0].wait()
    stores[1].wait()
    over_groups(lambda off: share_message(off).wait_recv())
    total = jnp.sum(shares[...], axis=0)
    for o in range(owned):
        pattern[:, o * row_tile : (o + 1) * row_tile] = total[o * STEPS : (o + 1) * STEPS]
    stores[2].start()

    over_groups(lambda off: share_message(off).wait_send())
    stores[2].wait()


def finish(e_in, h_in, p_in, e_out, h_out, p_out, e_held, h_held, p_held, in_sem, out_sem):
    held = ((e_in, e_held, e_out), (h_in, h_held, h_out), (p_in, p_held, p_out))
    loads = [pltpu.make_async_copy(a, b, in_sem.at[i]) for i, (a, b, _) in enumerate(held)]
    stores = [pltpu.make_async_copy(b, c, out_sem.at[i]) for i, (_, b, c) in enumerate(held)]
    for load in loads:
        load.start()
    for load, store in zip(loads, stores):
        load.wait()
        store.start()
    for store in stores:
        store.wait()


def on_device(
    sizes,
    electric, material, coef_keep, coef_curl, huygens_count, huygens_cells, band_tiles, radiation,
):
    cx, cy, cz = electric.shape[1:]
    hmax = huygens_cells.shape[-1]
    owned, row_tile = radiation.shape[0], radiation.shape[-1]
    n_gx, n_gy, n_af = sizes
    groups = n_gx * n_gy
    tiles = n_af * hmax // row_tile
    f32 = jnp.float32
    out_shape = (
        jax.ShapeDtypeStruct(electric.shape, f32),
        jax.ShapeDtypeStruct(electric.shape, f32),
        jax.ShapeDtypeStruct((STEPS, owned * row_tile), f32),
    )
    hbm = pl.BlockSpec(memory_space=pltpu.HBM)
    results = pl.pallas_call(
        functools.partial(kernel, sizes),
        out_shape=out_shape,
        in_specs=[hbm] * 8,
        out_specs=(hbm,) * 3,
        scratch_shapes=[
            pltpu.VMEM(electric.shape, f32),
            pltpu.VMEM(electric.shape, f32),
            pltpu.VMEM((STEPS, owned * row_tile), f32),
            pltpu.VMEM(material.shape, jnp.int32),
            pltpu.VMEM(coef_keep.shape, f32),
            pltpu.VMEM(coef_curl.shape, f32),
            pltpu.SMEM(huygens_count.shape, jnp.int32),
            pltpu.VMEM(huygens_cells.shape, jnp.int32),
            pltpu.SMEM(band_tiles.shape, jnp.int32),
            pltpu.VMEM((STEPS, FACES, cy, cz), f32),
            pltpu.VMEM((STEPS, GHOSTS, cy, cz), f32),
            pltpu.VMEM((2, cy, cz), f32),
            pltpu.VMEM((2, cx, cz), f32),
            pltpu.VMEM((2, cy, cz), f32),
            pltpu.VMEM((3, cx, cy, cz), f32),
            pltpu.VMEM((3, cx, cy, cz), f32),
            pltpu.VMEM((8, cz), f32),
            pltpu.VMEM((cz, hmax), jnp.bfloat16),
            pltpu.VMEM((cx * cy, hmax), f32),
            pltpu.VMEM((STEPS, tiles // 2, 16, row_tile), jnp.bfloat16),
            pltpu.VMEM(radiation.shape, jnp.bfloat16),
            pltpu.VMEM((groups, owned * STEPS, row_tile), f32),
            pltpu.SemaphoreType.DMA((STEPS, len(MESSAGES))),
            pltpu.SemaphoreType.DMA((STEPS, len(MESSAGES))),
            pltpu.SemaphoreType.DMA((STEPS, n_af)),
            pltpu.SemaphoreType.DMA((STEPS, n_af)),
            pltpu.SemaphoreType.DMA((groups,)),
            pltpu.SemaphoreType.DMA((groups,)),
            pltpu.SemaphoreType.DMA((8,)),
            pltpu.SemaphoreType.DMA((3,)),
        ],
        compiler_params=pltpu.CompilerParams(
            collective_id=0, has_side_effects=True, vmem_limit_bytes=62 * 1024 * 1024
        ),
    )(electric, material, coef_keep, coef_curl, huygens_count, huygens_cells, band_tiles, radiation)
    return pl.pallas_call(
        finish,
        out_shape=out_shape,
        in_specs=[hbm] * 3,
        out_specs=(hbm,) * 3,
        scratch_shapes=[pltpu.VMEM(shape.shape, f32) for shape in out_shape]
        + [pltpu.SemaphoreType.DMA((3,)), pltpu.SemaphoreType.DMA((3,))],
        compiler_params=pltpu.CompilerParams(vmem_limit_bytes=62 * 1024 * 1024),
    )(*results)


def solution(mesh):
    placed = (
        P(None, "gx", "gy", "af"),
        P("gx", "gy", "af"),
        P(),
        P(),
        P("gx", "gy", "af"),
        P("gx", "gy", "af", None),
        P(("gx", "gy"), "af", None),
        P("af", ("gx", "gy"), None, None, None, None),
    )
    sizes = (mesh.shape["gx"], mesh.shape["gy"], mesh.shape["af"])
    return jax.shard_map(
        functools.partial(on_device, sizes),
        mesh=mesh,
        in_specs=placed,
        out_specs=(P(None, "gx", "gy", "af"), P(None, "gx", "gy", "af"), P(None, "af")),
        check_vma=False,
    )
```

profile of v0, /device:TPU:0, one launch (start us, length us, event | category | flops | bytes accessed | tf_op | source)
XLA Modules:
  0.0 31.8 jit_solution(16160434650074612969)
XLA Ops:
  1.3 28.8 %shard_map.103 = (f32[3,16,8,128]{3,2,1,0:T(8,128)}, f32[3,16,8,128]{3,2,1,0:T(8,128)}, f32[4,256]{1,0:T(4,128)}) custom-call(f32[3,16,8,128]{3,2,1,0:T(8,128)} %electric_in.1, s32[16,8,128]{2,1,0:T(8,128)} %material_in.1, f32[3,16]{1,0:T(4,128)} %keep_in.1, f32[3,16]{1,0:T(4,128)} %curl_in.1, s32[1,1,1]{2,1,0:T(1,128)S(6)} %copy.11.count_in, ...), custom_call_target="tpu_custom_call" | custom-call | tf_op jit(solution)/shard_map/pallas_call | solution.py:403
  30.1 1.8 %shard_map.104 = (f32[3,16,8,128]{3,2,1,0:T(8,128)}, f32[3,16,8,128]{3,2,1,0:T(8,128)}, f32[4,256]{1,0:T(4,128)}) custom-call(f32[3,16,8,128]{3,2,1,0:T(8,128)} %get-tuple-element.6.e_in, f32[3,16,8,128]{3,2,1,0:T(8,128)} %get-tuple-element.7.h_in, f32[4,256]{1,0:T(4,128)} %get-tuple-element.8.p_in), custom_call_target="tpu_custom_call" | custom-call | tf_op jit(solution)/shard_map/pallas_call | solution.py:444
where the time goes:
time: 32 us; the launch traced here: 31.8 us
  Pallas kernels  30.6 us (96%)
  between operations  1.29 us (4%)
    pallas_call x1, Pallas kernels, on_device(): pl.pallas_call(functools.partial(kernel, sizes), out_shape=out_shape, in_...  28.8 us
    pallas_call x1, Pallas kernels, on_device(): pl.pallas_call(finish, out_shape=out_shape, in_specs=[hbm] * 3, out_specs...  1.75 us

commit v1 on v0

--- a/solution.py
+++ b/solution.py
@@ -370,14 +370,12 @@
     stores[2].wait()
 
 
-def finish(e_in, h_in, p_in, e_out, h_out, p_out, e_held, h_held, p_held, in_sem, out_sem):
-    held = ((e_in, e_held, e_out), (h_in, h_held, h_out), (p_in, p_held, p_out))
-    loads = [pltpu.make_async_copy(a, b, in_sem.at[i]) for i, (a, b, _) in enumerate(held)]
-    stores = [pltpu.make_async_copy(b, c, out_sem.at[i]) for i, (_, b, c) in enumerate(held)]
-    for load in loads:
-        load.start()
-    for load, store in zip(loads, stores):
-        load.wait()
+def finish(e_in, h_in, p_in, e_out, h_out, p_out, sem):
+    stores = [
+        pltpu.make_async_copy(src, dst, sem.at[i])
+        for i, (src, dst) in enumerate(((p_in, p_out), (e_in, e_out), (h_in, h_out)))
+    ]
+    for store in stores:
         store.start()
     for store in stores:
         store.wait()
@@ -400,11 +398,14 @@
         jax.ShapeDtypeStruct((STEPS, owned * row_tile), f32),
     )
     hbm = pl.BlockSpec(memory_space=pltpu.HBM)
+    anyw = pl.BlockSpec(memory_space=pl.ANY)
+    operands = [pltpu.with_memory_space_constraint(v, pltpu.HBM) for v in (electric, material, coef_keep, coef_curl)] + [huygens_count] + [
+        pltpu.with_memory_space_constraint(v, pltpu.HBM) for v in (huygens_cells, band_tiles, radiation)]
     results = pl.pallas_call(
         functools.partial(kernel, sizes),
         out_shape=out_shape,
         in_specs=[hbm] * 8,
-        out_specs=(hbm,) * 3,
+        out_specs=(anyw,) * 3,
         scratch_shapes=[
             pltpu.VMEM(electric.shape, f32),
             pltpu.VMEM(electric.shape, f32),
@@ -438,17 +439,16 @@
             pltpu.SemaphoreType.DMA((3,)),
         ],
         compiler_params=pltpu.CompilerParams(
-            collective_id=0, has_side_effects=True, vmem_limit_bytes=62 * 1024 * 1024
+            collective_id=0, has_side_effects=True, vmem_limit_bytes=16 * 1024 * 1024
         ),
-    )(electric, material, coef_keep, coef_curl, huygens_count, huygens_cells, band_tiles, radiation)
+    )(*operands)
     return pl.pallas_call(
         finish,
         out_shape=out_shape,
-        in_specs=[hbm] * 3,
+        in_specs=[anyw] * 3,
         out_specs=(hbm,) * 3,
-        scratch_shapes=[pltpu.VMEM(shape.shape, f32) for shape in out_shape]
-        + [pltpu.SemaphoreType.DMA((3,)), pltpu.SemaphoreType.DMA((3,))],
-        compiler_params=pltpu.CompilerParams(vmem_limit_bytes=62 * 1024 * 1024),
+        scratch_shapes=[pltpu.SemaphoreType.DMA((3,))],
+        compiler_params=pltpu.CompilerParams(vmem_limit_bytes=16 * 1024 * 1024),
     )(*results)
 
 

time: 32 us -> 31.3 us (0.978)
  Pallas kernels: 30.6 us -> 29.9 us
    pallas_call x1, Pallas kernels: 1.75 us -> 0.77 us  [on_device(): pl.pallas_call(finish, out_shape=out_shape, in_specs=[anyw] * 3, out_spec...]
where the time goes in v1:
time: 31.3 us; the launch traced here: 31.2 us
  Pallas kernels  29.9 us (96%)
  between operations  1.29 us (4%)
    pallas_call x1, Pallas kernels, on_device(): pl.pallas_call(functools.partial(kernel, sizes), out_shape=out_shape, in_...  29.1 us
    pallas_call x1, Pallas kernels, on_device(): pl.pallas_call(finish, out_shape=out_shape, in_specs=[anyw] * 3, out_spec...  0.77 us

profile of v1, /device:TPU:0, one launch (start us, length us, event | category | flops | bytes accessed | tf_op | source)
XLA Modules:
  0.0 31.2 jit_solution(13224525770200474044)
XLA Ops:
  1.3 29.1 %shard_map.103 = (f32[3,16,8,128]{3,2,1,0:T(8,128)S(1)}, f32[3,16,8,128]{3,2,1,0:T(8,128)S(1)}, f32[4,256]{1,0:T(4,128)S(1)}) custom-call(f32[3,16,8,128]{3,2,1,0:T(8,128)} %electric_in.1, s32[16,8,128]{2,1,0:T(8,128)} %material_in.1, f32[3,16]{1,0:T(4,128)} %keep_in.1, f32[3,16]{1,0:T(4,128)} %curl_in.1, s32[1,1,1]{2,1,0:T(1,128)S(6)} %copy.11.count_in, ...), custom_call_target="tpu_custom_call" | custom-call | tf_op jit(solution)/shard_map/pallas_call | solution.py:404
  30.4 0.8 %shard_map.104 = (f32[3,16,8,128]{3,2,1,0:T(8,128)}, f32[3,16,8,128]{3,2,1,0:T(8,128)}, f32[4,256]{1,0:T(4,128)}) custom-call(f32[3,16,8,128]{3,2,1,0:T(8,128)S(1)} %get-tuple-element.6.e_in, f32[3,16,8,128]{3,2,1,0:T(8,128)S(1)} %get-tuple-element.7.h_in, f32[4,256]{1,0:T(4,128)S(1)} %get-tuple-element.8.p_in), custom_call_target="tpu_custom_call" | custom-call | tf_op jit(solution)/shard_map/pallas_call | solution.py:445

commit v2 on v1

v2 whole, which is shorter than its diff:
```python
import functools
import itertools

import jax
import jax.numpy as jnp
from jax import lax
from jax.experimental import pallas as pl
from jax.experimental.pallas import tpu as pltpu
from jax.sharding import PartitionSpec as P

STEPS = 4
COURANT = 0.5
MESH = pl.DeviceIdType.MESH
f32, bf16 = jnp.float32, jnp.bfloat16

STEPS_TO = sorted(
    (d for d in itertools.product((-1, 0, 1), repeat=3) if any(d)),
    key=lambda d: (abs(d[2]), -abs(d[1]), abs(d[0])),
)


def kernel(
    sizes,
    electric_in, material_in, keep_in, curl_in, count_in, cells_in, band_in, radiation,
    e_end, h_end, p_end,
    e_out, h_out, pattern, material, coef_keep, coef_curl, count, cells, band,
    ef, gf, keep, gain, dz, ahead, behind, spread, low_mask,
    x_pack, y_pack, z_pack, x_ghost, y_ghost, z_ghost,
    table, zhot, rhot, rows, weights, shares,
    send_sem, recv_sem, row_send, row_recv, share_send, share_recv, load_sem, store_sem,
):
    n_gx, n_gy, n_af = sizes
    groups = n_gx * n_gy
    gx, gy, af = lax.axis_index("gx"), lax.axis_index("gy"), lax.axis_index("af")
    me = (gx, gy, af)
    group = gx * n_gy + gy
    cx, cy, cz = e_out.shape[1:]
    hmax = cells.shape[-1]
    row_tile = radiation.shape[-1]
    tiles = hmax // row_tile
    owned, entries, comps = radiation.shape[0], radiation.shape[2], radiation.shape[3]

    def exists(step):
        ok = None
        for at, d, n in zip(me, step, sizes):
            if d:
                term = (at + d >= 0) if d < 0 else (at + d < n)
                ok = term if ok is None else jnp.logical_and(ok, term)
        return ok

    def place(step):
        return tuple(jnp.clip(at + d, 0, n - 1) if d else at for at, d, n in zip(me, step, sizes))

    def back(step):
        return tuple(-d for d in step)

    def af_peer(off):
        return (gx, gy, lax.rem(af + off, n_af))

    def group_peer(off):
        other = lax.rem(group + off, groups)
        return (other // n_gy, lax.rem(other, n_gy), af)

    def over_groups(body):
        if groups <= 16:
            for off in range(1, groups):
                body(off)
        else:
            def step(off, carry):
                body(off)
                return carry
            lax.fori_loop(1, groups, step, 0)

    halo = STEPS
    planes = cx + 2 * halo
    own = pl.ds(halo, cx)
    wide = 2 * cz
    loads = [
        pltpu.make_async_copy(src, dst, load_sem.at[i])
        for i, (src, dst) in enumerate((
            (electric_in, ef.at[:, own, 0, :, pl.ds(0, cz)]), (material_in, material),
            (keep_in, coef_keep), (curl_in, coef_curl), (cells_in, cells), (count_in, count),
            (band_in, band), (radiation, weights),
        ))
    ]
    for load in loads:
        load.start()
    stores = [
        pltpu.make_async_copy(src, dst, store_sem.at[i])
        for i, (src, dst) in enumerate(((e_out, e_end), (h_out, h_end), (pattern, p_end)))
    ]

    barrier = pltpu.get_barrier_semaphore()
    for off in range(1, n_af):
        pl.semaphore_signal(barrier, inc=1, device_id=af_peer(off), device_id_type=MESH)
    over_groups(lambda off: pl.semaphore_signal(
        barrier, inc=1, device_id=group_peer(off), device_id_type=MESH))
    expected = jnp.int32(n_af - 1 + groups - 1)
    for step in STEPS_TO:
        if step[2] and (step[0] or step[1]):
            there = exists(step)
            expected = expected + there.astype(jnp.int32)

            @pl.when(there)
            def _(step=step):
                pl.semaphore_signal(barrier, inc=1, device_id=place(step), device_id_type=MESH)

    lane = lax.broadcasted_iota(jnp.int32, (cy, cz), 1)
    sub = lax.broadcasted_iota(jnp.int32, (cy, cz), 0)
    low_rows = sub < halo
    edge = 2 * halo

    at = lax.broadcasted_iota(jnp.int32, (cz, cz), 0)
    to = lax.broadcasted_iota(jnp.int32, (cz, cz), 1)
    packed_at = jnp.where(to < halo, to, jnp.where(to >= cz - halo, to - (cz - edge), -cx * cz))
    for i in range(cx):
        spread[:, i * cz : (i + 1) * cz] = (at == packed_at + i * edge).astype(f32).astype(bf16)

    loads[0].wait()
    loads[1].wait()

    def own_plane(c, i):
        if c < 3:
            return ef[c, halo + i, 0, :, 0:cz]
        return material[i].astype(f32)

    for c in range(4):
        for side, first in ((0, 0), (1, cx - halo)):
            for j in range(halo // 2):
                pair = [own_plane(c, first + 2 * j), own_plane(c, first + 2 * j + 1)]
                x_pack[side, c, j] = jnp.concatenate(pair, axis=0).astype(bf16)
        for j in range(cx // 4):
            four = [own_plane(c, 4 * j + r) for r in range(4)]
            turned = [pltpu.roll(four[1], halo, 0), pltpu.roll(four[3], halo, 0)]
            low = [jnp.where(low_rows, four[2 * r], turned[r]) for r in range(2)]
            high = [jnp.where(low_rows, turned[r], four[2 * r]) for r in range(2)]
            y_pack[0, c, j] = jnp.concatenate(low, axis=0).astype(bf16)
            y_pack[1, c, j] = jnp.concatenate(high, axis=0).astype(bf16)
    lines = [jnp.concatenate([own_plane(c, i) for i in range(cx)], axis=1) for c in range(4)]
    ends = lax.dot_general(
        jnp.concatenate(lines, axis=0).astype(bf16), spread[...],
        (((1,), (1,)), ((), ())), preferred_element_type=f32)
    z_pack[...] = ends.reshape(2, 2 * cy, cz).astype(bf16)

    def message(step):
        dx, dy, dz_ = step
        m = STEPS_TO.index(step)
        if dz_:
            src = z_pack
            dst = z_ghost.at[0 if dz_ < 0 else 1, (0, 2, 1)[dy], (0, 2, 1)[dx]]
        elif dy:
            side = 0 if dy < 0 else 1
            n = 1 if dx else cx // 4
            first = cx // 4 - 1 if dx > 0 else 0
            to = (1, 0, cx // 4 + 1)[dx]
            src = y_pack.at[side, :, pl.ds(first, n)]
            dst = y_ghost.at[side, :, pl.ds(to, n)]
        else:
            src = x_pack.at[1 if dx > 0 else 0]
            dst = x_ghost.at[0 if dx > 0 else 1]
        return pltpu.make_async_remote_copy(
            src_ref=src, dst_ref=dst, send_sem=send_sem.at[m], recv_sem=recv_sem.at[m],
            device_id=place(step), device_id_type=MESH,
        )

    pl.semaphore_wait(barrier, expected)
    for step in STEPS_TO:
        @pl.when(exists(step))
        def _(step=step):
            message(step).start()

    outside = float(coef_keep.shape[1])
    pair_row = lax.broadcasted_iota(jnp.int32, (2 * cy, cz), 0)
    for step in STEPS_TO:
        @pl.when(jnp.logical_not(exists(back(step))))
        def _(step=step):
            dx, dy, dz_ = step
            nothing = jnp.zeros((2 * cy, cz), bf16)
            beyond = jnp.full((2 * cy, cz), outside, bf16)
            if dz_:
                place_of = (0 if dz_ < 0 else 1, (0, 2, 1)[dy], (0, 2, 1)[dx])
                z_ghost[place_of + (0,)] = nothing
                z_ghost[place_of + (1,)] = jnp.where(
                    pair_row >= cy, outside, 0.0).astype(bf16)
            elif dy:
                n = 1 if dx else cx // 4
                to = (1, 0, cx // 4 + 1)[dx]
                for c in range(4):
                    for j in range(to, to + n):
                        y_ghost[0 if dy < 0 else 1, c, j] = nothing if c < 3 else beyond
            else:
                for c in range(4):
                    for j in range(halo // 2):
                        x_ghost[0 if dx > 0 else 1, c, j] = nothing if c < 3 else beyond

    for load in loads[2:-1]:
        load.wait()
    table[...] = jnp.zeros_like(table)
    mats = coef_keep.shape[1]
    table[0:3, 0:mats] = coef_keep[...]
    table[3:6, 0:mats] = -COURANT * coef_curl[...]
    factors = [jnp.broadcast_to(table[c : c + 1, :], (cy, cz)) for c in range(6)]

    def picked_factors(classes):
        return [
            jnp.take_along_axis(row, classes, axis=1, mode="promise_in_bounds") for row in factors
        ]

    def set_factors(p, t, classes):
        for c, value in enumerate(picked_factors(classes)):
            (keep if c < 3 else gain)[c % 3, p, t, :, 0:cz] = value

    for i in range(cx):
        set_factors(halo + i, 0, material[i])
    row_at = lax.broadcasted_iota(jnp.int32, (wide, wide), 0)
    col_at = lax.broadcasted_iota(jnp.int32, (wide, wide), 1)
    same = (row_at == col_at).astype(f32)
    ahead[...] = ((row_at == lax.rem(col_at + 1, wide)).astype(f32) - same).astype(bf16)
    behind[...] = (same - (lax.rem(row_at + 1, wide) == col_at).astype(f32)).astype(bf16)
    cell = jnp.broadcast_to(cells[...].reshape(1, hmax), (cz, hmax))
    zhot[...] = (lax.broadcasted_iota(jnp.int32, (cz, hmax), 0) == lax.rem(cell, cz)).astype(
        f32).astype(bf16)
    cell = jnp.broadcast_to(cells[...].reshape(1, hmax), (cx * cy, hmax))
    live = lax.broadcasted_iota(jnp.int32, (cx * cy, hmax), 1) < count[0, 0, 0]
    rhot[...] = jnp.logical_and(
        lax.broadcasted_iota(jnp.int32, (cx * cy, hmax), 0) == lax.div(cell, cz), live
    ).astype(f32)
    has_x = (gx > 0).astype(f32)
    has_y = (gy > 0).astype(f32)
    has_z = (af > 0).astype(f32)
    wide_lane = lax.broadcasted_iota(jnp.int32, (cy, wide), 1)
    wide_sub = lax.broadcasted_iota(jnp.int32, (cy, wide), 0)
    for x in range(2):
        for t in range(2):
            mask = jnp.where(wide_lane >= cz + cz // 2, has_z, 1.0)
            if t:
                mask = mask * jnp.where(wide_sub >= halo, has_y, 1.0)
            low_mask[2 * x + t] = mask * has_x if x else mask

    for step in STEPS_TO:
        @pl.when(exists(back(step)))
        def _(step=step):
            message(step).wait_recv()

    def as_classes(v):
        return v.astype(jnp.int32)

    for side, first in ((0, 0), (1, cx + halo)):
        for j in range(halo // 2):
            for c in range(4):
                pair = x_ghost[side, c, j].astype(f32)
                for r in range(2):
                    p = first + 2 * j + r
                    v = pair[r * cy : (r + 1) * cy]
                    if c < 3:
                        ef[c, p, 0, :, 0:cz] = v
                    else:
                        set_factors(p, 0, as_classes(v))
    for j in range(planes // 4):
        for c in range(4):
            above = y_ghost[0, c, j].astype(f32)
            below = y_ghost[1, c, j].astype(f32)
            for r in range(2):
                up, down = above[r * cy : (r + 1) * cy], below[r * cy : (r + 1) * cy]
                both = (
                    jnp.where(low_rows, up, down),
                    pltpu.roll(jnp.where(low_rows, down, up), halo, 0),
                )
                for q in range(2):
                    p = 4 * j + 2 * r + q
                    if c < 3:
                        ef[c, p, 1, :, 0:cz] = both[q]
                    else:
                        set_factors(p, 1, as_classes(both[q]))
    from_above = lax.rem(lane, edge) < halo

    def ends_of(c, t, chunk):
        def joined(dyi, dxi):
            at = (slice((c % 2) * cy, (c % 2 + 1) * cy), slice(None))
            return jnp.where(
                from_above, z_ghost[0, dyi, dxi, c // 2][at].astype(f32),
                z_ghost[1, dyi, dxi, c // 2][at].astype(f32))

        def over_x(dyi):
            if chunk == 0:
                return joined(dyi, 0)
            return jnp.where(lane < cz // 2, joined(dyi, 1), joined(dyi, 2))

        return over_x(0) if t == 0 else jnp.where(low_rows, over_x(1), over_x(2))

    for chunk in range(2):
        if chunk == 0:
            blocks = [(0, [halo + i for i in range(cx)])]
        else:
            blocks = [(0, [cx + halo + i for i in range(halo)]), (cx - halo, list(range(halo)))]
        field = jnp.concatenate(
            [ends_of(c, t, chunk) for c in range(3) for t in range(2)], axis=0).astype(bf16)
        found = [picked_factors(as_classes(ends_of(3, t, chunk))) for t in range(2)]
        factor = jnp.concatenate([found[t][c] for c in range(6) for t in range(2)], axis=0)
        rough = factor.astype(bf16)
        rest = (factor - rough.astype(f32)).astype(bf16)
        for first, where_to in blocks:
            part = spread[:, first * cz : (first + len(where_to)) * cz]
            a = jnp.dot(field, part, preferred_element_type=f32)
            b = jnp.dot(rough, part, preferred_element_type=f32)
            b = b + jnp.dot(rest, part, preferred_element_type=f32)
            for i, p in enumerate(where_to):
                cols = slice(i * cz, (i + 1) * cz)
                for t in range(2):
                    for c in range(3):
                        at_row = (2 * c + t) * cy
                        ef[c, p, t, :, cz:wide] = a[at_row : at_row + cy, cols]
                        keep[c, p, t, :, cz:wide] = b[at_row : at_row + cy, cols]
                        at_row += 6 * cy
                        gain[c, p, t, :, cz:wide] = b[at_row : at_row + cy, cols]

    def row_message(t, off):
        mine = rows.at[t, pl.ds(af * (tiles // 2), tiles // 2)]
        return pltpu.make_async_remote_copy(
            src_ref=mine, dst_ref=mine,
            send_sem=row_send.at[t, off], recv_sem=row_recv.at[t, off],
            device_id=af_peer(off), device_id_type=MESH,
        )

    def up_y(v):
        r = [pltpu.roll(tile, cy - 1, 0) for tile in v]
        last = wide_sub == cy - 1
        return [jnp.where(last, r[1], r[0]), jnp.where(last, r[0], r[1])]

    def down_y(v):
        r = [pltpu.roll(tile, 1, 0) for tile in v]
        first = wide_sub == 0
        return [jnp.where(first, r[1], r[0]), jnp.where(first, r[0], r[1])]

    def along_z(ref, c, first, n, matrix, width):
        v = ref[c, first : first + n].reshape(n * 2 * cy, wide)
        rough = v.astype(bf16)
        rest = (v - rough.astype(f32)).astype(bf16)
        change = jnp.dot(rough, matrix[:, 0:width], preferred_element_type=f32)
        change = change + jnp.dot(rest, matrix[:, 0:width], preferred_element_type=f32)
        dz[c, first : first + n, :, :, 0:width] = change.reshape(n, 2, cy, width)

    for t in range(STEPS):
        first, last = t, planes - 2 - t
        for c in range(2):
            along_z(ef, c, first, last - first + 1, ahead, wide)
        for p in range(first, last + 1):
            ex, ey, ez = [[ef[c, p, y] for y in range(2)] for c in range(3)]
            ez_y, ex_y = up_y(ez), up_y(ex)
            for y in range(2):
                change = (
                    (ez_y[y] - ez[y]) - dz[1, p, y],
                    dz[0, p, y] - (ef[2, p + 1, y] - ez[y]),
                    (ef[1, p + 1, y] - ey[y]) - (ex_y[y] - ex[y]),
                )
                mask = low_mask[(2 if p < halo else 0) + y]
                for c in range(3):
                    new = change[c] * mask
                    if t:
                        new = gf[c, p, y] + new
                    gf[c, p, y] = new
        first = t + 1
        end = t + 1 == STEPS
        width = cz if end else wide
        for c in range(2):
            along_z(gf, c, first, last - first + 1, behind, width)
        for p in range(first, last + 1):
            hx, hz = [[gf[c, p, y] for y in range(2)] for c in (0, 2)]
            hx_y, hz_y = down_y(hx), down_y(hz)
            for y in range(1 if end else 2):
                w = slice(0, width)
                change = (
                    (hz[y] - hz_y[y])[:, w] - dz[1, p, y, :, w],
                    dz[0, p, y, :, w] - (hz[y] - gf[2, p - 1, y])[:, w],
                    (gf[1, p, y] - gf[1, p - 1, y])[:, w] - (hx[y] - hx_y[y])[:, w],
                )
                for c in range(3):
                    new = keep[c, p, y, :, w] * ef[c, p, y, :, w] + gain[c, p, y, :, w] * change[c]
                    if end:
                        e_out[c, p - halo] = new
                        h_out[c, p - halo] = -COURANT * gf[c, p, 0, :, w]
                    else:
                        ef[c, p, y] = new
        if end:
            stores[0].start()
            stores[1].start()

        picked = []
        for k in range(comps):
            if end:
                field = (e_out if k < 3 else h_out)[k % 3]
            else:
                field = (ef if k < 3 else gf)[k % 3, halo : halo + cx, 0, :, 0:cz]
            values = field.reshape(cx * cy, cz)
            if k >= 3 and not end:
                values = -COURANT * values
            column = jnp.dot(values.astype(bf16), zhot[...], preferred_element_type=f32)
            picked.append(jnp.sum(column * rhot[...], axis=0, keepdims=True))
        picked.append(jnp.zeros((8 - comps, hmax), jnp.float32))
        picked = jnp.concatenate(picked, axis=0)
        for q in range(tiles // 2):
            at = 2 * q * row_tile
            pair = [picked[:, at : at + row_tile], picked[:, at + row_tile : at + 2 * row_tile]]
            rows[t, af * (tiles // 2) + q] = jnp.concatenate(pair, axis=0).astype(jnp.bfloat16)
        for off in range(1, n_af):
            row_message(t, off).start()

    loads[-1].wait()
    for t in range(STEPS):
        for off in range(1, n_af):
            row_message(t, off).wait_recv()

    sums = []
    for o in range(owned):
        total = None
        for n in range(entries):
            tile = band[0, o, n]
            pairs = [rows[t, tile // 2].astype(jnp.float32) for t in range(STEPS)]
            odd = lax.rem(tile, 2)
            segment = jnp.concatenate(
                [jnp.where(odd == 1, pair[8:], pair[:8]) for pair in pairs], axis=0)
            term = lax.dot_general(
                segment.astype(jnp.bfloat16),
                weights[o, 0, n].reshape(comps * row_tile, row_tile),
                (((1,), (1,)), ((), ())),
                preferred_element_type=jnp.float32,
            )
            total = term if total is None else total + term
        for t in range(STEPS):
            own = total[t * 8 : t * 8 + 1, 0:row_tile]
            for k in range(1, comps):
                own = own + total[t * 8 + k : t * 8 + k + 1, k * row_tile : (k + 1) * row_tile]
            sums.append(own)
    shares[group] = jnp.concatenate(sums, axis=0)

    def share_message(off):
        return pltpu.make_async_remote_copy(
            src_ref=shares.at[group], dst_ref=shares.at[group],
            send_sem=share_send.at[off], recv_sem=share_recv.at[off],
            device_id=group_peer(off), device_id_type=MESH,
        )

    over_groups(lambda off: share_message(off).start())
    for t in range(STEPS):
        for off in range(1, n_af):
            row_message(t, off).wait_send()
    for step in STEPS_TO:
        @pl.when(exists(step))
        def _(step=step):
            message(step).wait_send()
    stores[0].wait()
    stores[1].wait()
    over_groups(lambda off: share_message(off).wait_recv())
    total = jnp.sum(shares[...], axis=0)
    for o in range(owned):
        pattern[:, o * row_tile : (o + 1) * row_tile] = total[o * STEPS : (o + 1) * STEPS]
    stores[2].start()

    over_groups(lambda off: share_message(off).wait_send())
    stores[2].wait()


def finish(e_in, h_in, p_in, e_out, h_out, p_out, sem):
    stores = [
        pltpu.make_async_copy(src, dst, sem.at[i])
        for i, (src, dst) in enumerate(((p_in, p_out), (e_in, e_out), (h_in, h_out)))
    ]
    for store in stores:
        store.start()
    for store in stores:
        store.wait()


def on_device(
    sizes,
    electric, material, coef_keep, coef_curl, huygens_count, huygens_cells, band_tiles, radiation,
):
    cx, cy, cz = electric.shape[1:]
    hmax = huygens_cells.shape[-1]
    owned, row_tile = radiation.shape[0], radiation.shape[-1]
    n_gx, n_gy, n_af = sizes
    groups = n_gx * n_gy
    tiles = n_af * hmax // row_tile
    planes = cx + 2 * STEPS
    out_shape = (
        jax.ShapeDtypeStruct(electric.shape, f32),
        jax.ShapeDtypeStruct(electric.shape, f32),
        jax.ShapeDtypeStruct((STEPS, owned * row_tile), f32),
    )
    hbm = pl.BlockSpec(memory_space=pltpu.HBM)
    anyw = pl.BlockSpec(memory_space=pl.ANY)
    operands = [pltpu.with_memory_space_constraint(v, pltpu.HBM) for v in (electric, material, coef_keep, coef_curl)] + [huygens_count] + [
        pltpu.with_memory_space_constraint(v, pltpu.HBM) for v in (huygens_cells, band_tiles, radiation)]
    results = pl.pallas_call(
        functools.partial(kernel, sizes),
        out_shape=out_shape,
        in_specs=[hbm] * 8,
        out_specs=(anyw,) * 3,
        scratch_shapes=[
            pltpu.VMEM(electric.shape, f32),
            pltpu.VMEM(electric.shape, f32),
            pltpu.VMEM((STEPS, owned * row_tile), f32),
            pltpu.VMEM(material.shape, jnp.int32),
            pltpu.VMEM(coef_keep.shape, f32),
            pltpu.VMEM(coef_curl.shape, f32),
            pltpu.SMEM(huygens_count.shape, jnp.int32),
            pltpu.VMEM(huygens_cells.shape, jnp.int32),
            pltpu.SMEM(band_tiles.shape, jnp.int32),
            pltpu.VMEM((3, planes, 2, cy, 2 * cz), f32),
            pltpu.VMEM((3, planes, 2, cy, 2 * cz), f32),
            pltpu.VMEM((3, planes, 2, cy, 2 * cz), f32),
            pltpu.VMEM((3, planes, 2, cy, 2 * cz), f32),
            pltpu.VMEM((2, planes, 2, cy, 2 * cz), f32),
            pltpu.VMEM((2 * cz, 2 * cz), bf16),
            pltpu.VMEM((2 * cz, 2 * cz), bf16),
            pltpu.VMEM((cz, cx * cz), bf16),
            pltpu.VMEM((4, cy, 2 * cz), f32),
            pltpu.VMEM((2, 4, STEPS // 2, 2 * cy, cz), bf16),
            pltpu.VMEM((2, 4, cx // 4, 2 * cy, cz), bf16),
            pltpu.VMEM((2, 2 * cy, cz), bf16),
            pltpu.VMEM((2, 4, STEPS // 2, 2 * cy, cz), bf16),
            pltpu.VMEM((2, 4, planes // 4, 2 * cy, cz), bf16),
            pltpu.VMEM((2, 3, 3, 2, 2 * cy, cz), bf16),
            pltpu.VMEM((8, cz), f32),
            pltpu.VMEM((cz, hmax), jnp.bfloat16),
            pltpu.VMEM((cx * cy, hmax), f32),
            pltpu.VMEM((STEPS, tiles // 2, 16, row_tile), jnp.bfloat16),
            pltpu.VMEM(radiation.shape, jnp.bfloat16),
            pltpu.VMEM((groups, owned * STEPS, row_tile), f32),
            pltpu.SemaphoreType.DMA((len(STEPS_TO),)),
            pltpu.SemaphoreType.DMA((len(STEPS_TO),)),
            pltpu.SemaphoreType.DMA((STEPS, n_af)),
            pltpu.SemaphoreType.DMA((STEPS, n_af)),
            pltpu.SemaphoreType.DMA((groups,)),
            pltpu.SemaphoreType.DMA((groups,)),
            pltpu.SemaphoreType.DMA((8,)),
            pltpu.SemaphoreType.DMA((3,)),
        ],
        compiler_params=pltpu.CompilerParams(
            collective_id=0, has_side_effects=True, vmem_limit_bytes=24 * 1024 * 1024
        ),
    )(*operands)
    return pl.pallas_call(
        finish,
        out_shape=out_shape,
        in_specs=[anyw] * 3,
        out_specs=(hbm,) * 3,
        scratch_shapes=[pltpu.SemaphoreType.DMA((3,))],
        compiler_params=pltpu.CompilerParams(vmem_limit_bytes=16 * 1024 * 1024),
    )(*results)


def solution(mesh):
    placed = (
        P(None, "gx", "gy", "af"),
        P("gx", "gy", "af"),
        P(),
        P(),
        P("gx", "gy", "af"),
        P("gx", "gy", "af", None),
        P(("gx", "gy"), "af", None),
        P("af", ("gx", "gy"), None, None, None, None),
    )
    sizes = (mesh.shape["gx"], mesh.shape["gy"], mesh.shape["af"])
    return jax.shard_map(
        functools.partial(on_device, sizes),
        mesh=mesh,
        in_specs=placed,
        out_specs=(P(None, "gx", "gy", "af"), P(None, "gx", "gy", "af"), P(None, "af")),
        check_vma=False,
    )
```

time: 31.3 us -> 26.2 us (0.84)
  Pallas kernels: 29.9 us -> 24.8 us
    pallas_call x1, Pallas kernels: 29.1 us -> 24 us  [on_device(): pl.pallas_call(functools.partial(kernel, sizes), out_shape=out_shape, in_...]
where the time goes in v2:
time: 26.2 us; the launch traced here: 26.1 us
  Pallas kernels  24.8 us (95%)
  between operations  1.29 us (5%)
    pallas_call x1, Pallas kernels, on_device(): pl.pallas_call(functools.partial(kernel, sizes), out_shape=out_shape, in_...  24 us
    pallas_call x1, Pallas kernels, on_device(): pl.pallas_call(finish, out_shape=out_shape, in_specs=[anyw] * 3, out_spec...  0.77 us

profile of v2, /device:TPU:0, one launch (start us, length us, event | category | flops | bytes accessed | tf_op | source)
XLA Modules:
  0.0 26.1 jit_solution(2817865511713955564)
XLA Ops:
  1.3 24.0 %shard_map.103 = (f32[3,16,8,128]{3,2,1,0:T(8,128)S(1)}, f32[3,16,8,128]{3,2,1,0:T(8,128)S(1)}, f32[4,256]{1,0:T(4,128)S(1)}) custom-call(f32[3,16,8,128]{3,2,1,0:T(8,128)} %electric_in.1, s32[16,8,128]{2,1,0:T(8,128)} %material_in.1, f32[3,16]{1,0:T(4,128)} %keep_in.1, f32[3,16]{1,0:T(4,128)} %curl_in.1, s32[1,1,1]{2,1,0:T(1,128)S(6)} %copy.11.count_in, ...), custom_call_target="tpu_custom_call" | custom-call | tf_op jit(solution)/shard_map/pallas_call | solution.py:494
  25.3 0.8 %shard_map.104 = (f32[3,16,8,128]{3,2,1,0:T(8,128)}, f32[3,16,8,128]{3,2,1,0:T(8,128)}, f32[4,256]{1,0:T(4,128)}) custom-call(f32[3,16,8,128]{3,2,1,0:T(8,128)S(1)} %get-tuple-element.6.e_in, f32[3,16,8,128]{3,2,1,0:T(8,128)S(1)} %get-tuple-element.7.h_in, f32[4,256]{1,0:T(4,128)S(1)} %get-tuple-element.8.p_in), custom_call_target="tpu_custom_call" | custom-call | tf_op jit(solution)/shard_map/pallas_call | solution.py:543

commit v3 on v2

--- a/solution.py
+++ b/solution.py
@@ -17,15 +17,16 @@
     (d for d in itertools.product((-1, 0, 1), repeat=3) if any(d)),
     key=lambda d: (abs(d[2]), -abs(d[1]), abs(d[0])),
 )
+MESSAGES = [(d, 1) for d in STEPS_TO if d[1] and not d[2]] + [(d, 0) for d in STEPS_TO]
 
 
 def kernel(
     sizes,
     electric_in, material_in, keep_in, curl_in, count_in, cells_in, band_in, radiation,
-    e_end, h_end, p_end,
-    e_out, h_out, pattern, material, coef_keep, coef_curl, count, cells, band,
+    e_end, h_end, pattern,
+    e_out, h_out, material, coef_keep, coef_curl, count, cells, band,
     ef, gf, keep, gain, dz, ahead, behind, spread, low_mask,
-    x_pack, y_pack, z_pack, x_ghost, y_ghost, z_ghost,
+    x_pack, y_pack, z_pack, zy_pack, x_ghost, y_ghost, z_ghost, zy_ghost,
     table, zhot, rhot, rows, weights, shares,
     send_sem, recv_sem, row_send, row_recv, share_send, share_recv, load_sem, store_sem,
 ):
@@ -83,11 +84,9 @@
             (band_in, band), (radiation, weights),
         ))
     ]
-    for load in loads:
-        load.start()
     stores = [
         pltpu.make_async_copy(src, dst, store_sem.at[i])
-        for i, (src, dst) in enumerate(((e_out, e_end), (h_out, h_end), (pattern, p_end)))
+        for i, (src, dst) in enumerate(((e_out, e_end), (h_out, h_end)))
     ]
 
     barrier = pltpu.get_barrier_semaphore()
@@ -105,6 +104,9 @@
             def _(step=step):
                 pl.semaphore_signal(barrier, inc=1, device_id=place(step), device_id_type=MESH)
 
+    for load in loads[:-1]:
+        load.start()
+
     lane = lax.broadcasted_iota(jnp.int32, (cy, cz), 1)
     sub = lax.broadcasted_iota(jnp.int32, (cy, cz), 0)
     low_rows = sub < halo
@@ -125,10 +127,6 @@
         return material[i].astype(f32)
 
     for c in range(4):
-        for side, first in ((0, 0), (1, cx - halo)):
-            for j in range(halo // 2):
-                pair = [own_plane(c, first + 2 * j), own_plane(c, first + 2 * j + 1)]
-                x_pack[side, c, j] = jnp.concatenate(pair, axis=0).astype(bf16)
         for j in range(cx // 4):
             four = [own_plane(c, 4 * j + r) for r in range(4)]
             turned = [pltpu.roll(four[1], halo, 0), pltpu.roll(four[3], halo, 0)]
@@ -136,38 +134,66 @@
             high = [jnp.where(low_rows, turned[r], four[2 * r]) for r in range(2)]
             y_pack[0, c, j] = jnp.concatenate(low, axis=0).astype(bf16)
             y_pack[1, c, j] = jnp.concatenate(high, axis=0).astype(bf16)
+    def message(m):
+        (dx, dy, dz_), part = MESSAGES[m]
+        side = 0 if dy < 0 else 1
+        if dz_ and dy:
+            src = zy_pack.at[side]
+            dst = zy_ghost.at[0 if dz_ < 0 else 1, side, (0, 2, 1)[dx]]
+        elif dz_:
+            src = z_pack
+            dst = z_ghost.at[0 if dz_ < 0 else 1, (0, 2, 1)[dx]]
+        elif dy:
+            n = 1 if dx else cx // 4
+            first = cx // 4 - 1 if dx > 0 else 0
+            to = (1, 0, cx // 4 + 1)[dx]
+            what = pl.ds(3, 1) if part else pl.ds(0, 3)
+            src = y_pack.at[side, what, pl.ds(first, n)]
+            dst = y_ghost.at[side, what, pl.ds(to, n)]
+        else:
+            src = x_pack.at[1 if dx > 0 else 0]
+            dst = x_ghost.at[0 if dx > 0 else 1]
+        return pltpu.make_async_remote_copy(
+            src_ref=src, dst_ref=dst, send_sem=send_sem.at[m], recv_sem=recv_sem.at[m],
+            device_id=place((dx, dy, dz_)), device_id_type=MESH,
+        )
+
+    def send(wanted):
+        for m, (step, _) in enumerate(MESSAGES):
+            if wanted(step):
+                @pl.when(exists(step))
+                def _(m=m):
+                    message(m).start()
+
+    pl.semaphore_wait(barrier, expected)
+    send(lambda d: d[1] and not d[2])
+    for c in range(4):
+        for side, first in ((0, 0), (1, cx - halo)):
+            for j in range(halo // 2):
+                pair = [own_plane(c, first + 2 * j), own_plane(c, first + 2 * j + 1)]
+                x_pack[side, c, j] = jnp.concatenate(pair, axis=0).astype(bf16)
+    send(lambda d: not d[1] and not d[2])
     lines = [jnp.concatenate([own_plane(c, i) for i in range(cx)], axis=1) for c in range(4)]
     ends = lax.dot_general(
         jnp.concatenate(lines, axis=0).astype(bf16), spread[...],
         (((1,), (1,)), ((), ())), preferred_element_type=f32)
     z_pack[...] = ends.reshape(2, 2 * cy, cz).astype(bf16)
-
-    def message(step):
-        dx, dy, dz_ = step
-        m = STEPS_TO.index(step)
-        if dz_:
-            src = z_pack
-            dst = z_ghost.at[0 if dz_ < 0 else 1, (0, 2, 1)[dy], (0, 2, 1)[dx]]
-        elif dy:
-            side = 0 if dy < 0 else 1
-            n = 1 if dx else cx // 4
-            first = cx // 4 - 1 if dx > 0 else 0
-            to = (1, 0, cx // 4 + 1)[dx]
-            src = y_pack.at[side, :, pl.ds(first, n)]
-            dst = y_ghost.at[side, :, pl.ds(to, n)]
-        else:
-            src = x_pack.at[1 if dx > 0 else 0]
-            dst = x_ghost.at[0 if dx > 0 else 1]
-        return pltpu.make_async_remote_copy(
-            src_ref=src, dst_ref=dst, send_sem=send_sem.at[m], recv_sem=recv_sem.at[m],
-            device_id=place(step), device_id_type=MESH,
-        )
-
-    pl.semaphore_wait(barrier, expected)
-    for step in STEPS_TO:
-        @pl.when(exists(step))
-        def _(step=step):
-            message(step).start()
+    line = [ends[c * cy : (c + 1) * cy] for c in range(4)]
+    turned = [pltpu.roll(line[1], halo, 0), pltpu.roll(line[3], halo, 0)]
+    low = [jnp.where(low_rows, line[2 * r], turned[r]) for r in range(2)]
+    high = [jnp.where(low_rows, turned[r], line[2 * r]) for r in range(2)]
+    zy_pack[0] = jnp.concatenate(low, axis=0).astype(bf16)
+    zy_pack[1] = jnp.concatenate(high, axis=0).astype(bf16)
+
+    send(lambda d: d[2])
+    loads[-1].start()
+
+    def receive(wanted):
+        for m, (step, part) in enumerate(MESSAGES):
+            if wanted(step, part):
+                @pl.when(exists(back(step)))
+                def _(m=m):
+                    message(m).wait_recv()
 
     outside = float(coef_keep.shape[1])
     pair_row = lax.broadcasted_iota(jnp.int32, (2 * cy, cz), 0)
@@ -177,8 +203,13 @@
             dx, dy, dz_ = step
             nothing = jnp.zeros((2 * cy, cz), bf16)
             beyond = jnp.full((2 * cy, cz), outside, bf16)
-            if dz_:
-                place_of = (0 if dz_ < 0 else 1, (0, 2, 1)[dy], (0, 2, 1)[dx])
+            if dz_ and dy:
+                first = cy + halo if dy < 0 else cy
+                is_class = jnp.logical_and(pair_row >= first, pair_row < first + halo)
+                zy_ghost[0 if dz_ < 0 else 1, 0 if dy < 0 else 1, (0, 2, 1)[dx]] = jnp.where(
+                    is_class, outside, 0.0).astype(bf16)
+            elif dz_:
+                place_of = (0 if dz_ < 0 else 1, (0, 2, 1)[dx])
                 z_ghost[place_of + (0,)] = nothing
                 z_ghost[place_of + (1,)] = jnp.where(
                     pair_row >= cy, outside, 0.0).astype(bf16)
@@ -217,13 +248,17 @@
     same = (row_at == col_at).astype(f32)
     ahead[...] = ((row_at == lax.rem(col_at + 1, wide)).astype(f32) - same).astype(bf16)
     behind[...] = (same - (lax.rem(row_at + 1, wide) == col_at).astype(f32)).astype(bf16)
-    cell = jnp.broadcast_to(cells[...].reshape(1, hmax), (cz, hmax))
-    zhot[...] = (lax.broadcasted_iota(jnp.int32, (cz, hmax), 0) == lax.rem(cell, cz)).astype(
+    deep = 4 * cz
+    high = cx * cy // 4
+    cell = jnp.broadcast_to(cells[...].reshape(1, hmax), (deep, hmax))
+    wanted = lax.div(cell, high * cz) * cz + lax.rem(cell, cz)
+    zhot[...] = (lax.broadcasted_iota(jnp.int32, (deep, hmax), 0) == wanted).astype(
         f32).astype(bf16)
-    cell = jnp.broadcast_to(cells[...].reshape(1, hmax), (cx * cy, hmax))
-    live = lax.broadcasted_iota(jnp.int32, (cx * cy, hmax), 1) < count[0, 0, 0]
+    cell = jnp.broadcast_to(cells[...].reshape(1, hmax), (high, hmax))
+    slot = lax.broadcasted_iota(jnp.int32, (high, hmax), 1)
     rhot[...] = jnp.logical_and(
-        lax.broadcasted_iota(jnp.int32, (cx * cy, hmax), 0) == lax.div(cell, cz), live
+        lax.broadcasted_iota(jnp.int32, (high, hmax), 0) == lax.rem(lax.div(cell, cz), high),
+        slot < count[0, 0, 0],
     ).astype(f32)
     has_x = (gx > 0).astype(f32)
     has_y = (gy > 0).astype(f32)
@@ -237,14 +272,22 @@
                 mask = mask * jnp.where(wide_sub >= halo, has_y, 1.0)
             low_mask[2 * x + t] = mask * has_x if x else mask
 
-    for step in STEPS_TO:
-        @pl.when(exists(back(step)))
-        def _(step=step):
-            message(step).wait_recv()
-
     def as_classes(v):
         return v.astype(jnp.int32)
 
+    def beside_y(c, use):
+        for j in range(planes // 4):
+            above = y_ghost[0, c, j].astype(f32)
+            below = y_ghost[1, c, j].astype(f32)
+            for r in range(2):
+                up, down = above[r * cy : (r + 1) * cy], below[r * cy : (r + 1) * cy]
+                use(4 * j + 2 * r, jnp.where(low_rows, up, down))
+                use(4 * j + 2 * r + 1, pltpu.roll(jnp.where(low_rows, down, up), halo, 0))
+
+    receive(lambda d, part: d[1] and part)
+    beside_y(3, lambda p, v: set_factors(p, 1, as_classes(v)))
+
+    receive(lambda d, part: d[0] and not d[1] and not d[2])
     for side, first in ((0, 0), (1, cx + halo)):
         for j in range(halo // 2):
             for c in range(4):
@@ -256,37 +299,30 @@
                         ef[c, p, 0, :, 0:cz] = v
                     else:
                         set_factors(p, 0, as_classes(v))
-    for j in range(planes // 4):
-        for c in range(4):
-            above = y_ghost[0, c, j].astype(f32)
-            below = y_ghost[1, c, j].astype(f32)
-            for r in range(2):
-                up, down = above[r * cy : (r + 1) * cy], below[r * cy : (r + 1) * cy]
-                both = (
-                    jnp.where(low_rows, up, down),
-                    pltpu.roll(jnp.where(low_rows, down, up), halo, 0),
-                )
-                for q in range(2):
-                    p = 4 * j + 2 * r + q
-                    if c < 3:
-                        ef[c, p, 1, :, 0:cz] = both[q]
-                    else:
-                        set_factors(p, 1, as_classes(both[q]))
+
+    receive(lambda d, part: d[2])
     from_above = lax.rem(lane, edge) < halo
 
     def ends_of(c, t, chunk):
-        def joined(dyi, dxi):
-            at = (slice((c % 2) * cy, (c % 2 + 1) * cy), slice(None))
-            return jnp.where(
-                from_above, z_ghost[0, dyi, dxi, c // 2][at].astype(f32),
-                z_ghost[1, dyi, dxi, c // 2][at].astype(f32))
-
-        def over_x(dyi):
-            if chunk == 0:
-                return joined(dyi, 0)
-            return jnp.where(lane < cz // 2, joined(dyi, 1), joined(dyi, 2))
-
-        return over_x(0) if t == 0 else jnp.where(low_rows, over_x(1), over_x(2))
+        half = slice((c % 2) * cy, (c % 2 + 1) * cy)
+        pair = slice((c // 2) * cy, (c // 2 + 1) * cy)
+
+        def joined(dxi):
+            if t == 0:
+                above, below = [z_ghost[side, dxi, c // 2].astype(f32)[half] for side in range(2)]
+                return jnp.where(from_above, above, below)
+            out = []
+            for side in range(2):
+                up, down = [zy_ghost[side, y, dxi].astype(f32)[pair] for y in range(2)]
+                if c % 2:
+                    out.append(pltpu.roll(jnp.where(low_rows, down, up), halo, 0))
+                else:
+                    out.append(jnp.where(low_rows, up, down))
+            return jnp.where(from_above, out[0], out[1])
+
+        if chunk == 0:
+            return joined(0)
+        return jnp.where(lane < cz // 2, joined(1), joined(2))
 
     for chunk in range(2):
         if chunk == 0:
@@ -314,6 +350,13 @@
                         at_row += 6 * cy
                         gain[c, p, t, :, cz:wide] = b[at_row : at_row + cy, cols]
 
+    receive(lambda d, part: d[1] and not d[2] and not part)
+    for c in range(3):
+        def put(p, v, c=c):
+            ef[c, p, 1, :, 0:cz] = v
+
+        beside_y(c, put)
+
     def row_message(t, off):
         mine = rows.at[t, pl.ds(af * (tiles // 2), tiles // 2)]
         return pltpu.make_async_remote_copy(
@@ -332,16 +375,44 @@
         first = wide_sub == 0
         return [jnp.where(first, r[1], r[0]), jnp.where(first, r[0], r[1])]
 
-    def along_z(ref, c, first, n, matrix, width):
-        v = ref[c, first : first + n].reshape(n * 2 * cy, wide)
+    def along_z(ref, c, first, n, matrix, width, tiles_y=2):
+        v = ref[c, first : first + n, 0:tiles_y].reshape(n * tiles_y * cy, wide)
         rough = v.astype(bf16)
         rest = (v - rough.astype(f32)).astype(bf16)
         change = jnp.dot(rough, matrix[:, 0:width], preferred_element_type=f32)
         change = change + jnp.dot(rest, matrix[:, 0:width], preferred_element_type=f32)
-        dz[c, first : first + n, :, :, 0:width] = change.reshape(n, 2, cy, width)
-
+        dz[c, first : first + n, 0:tiles_y, :, 0:width] = change.reshape(n, tiles_y, cy, width)
+
+    def pick(compact, field):
+        lines = []
+        for k in range(3):
+            if compact is not None:
+                values = compact[k]
+            else:
+                values = field[k, halo : halo + cx, 0, :, 0:cz]
+            quarters = values.reshape(4, high, cz)
+            lines.append(jnp.concatenate([quarters[q] for q in range(4)], axis=1))
+        column = jnp.dot(
+            jnp.concatenate(lines, axis=0).astype(bf16), zhot[...], preferred_element_type=f32)
+        return [
+            jnp.sum(column[k * high : (k + 1) * high] * rhot[...], axis=0, keepdims=True)
+            for k in range(3)
+        ]
+
+    def send_rows(t, electric_rows, magnetic_rows):
+        picked = electric_rows + [-COURANT * row for row in magnetic_rows]
+        picked = jnp.concatenate(picked + [jnp.zeros((8 - comps, hmax), f32)], axis=0)
+        for q in range(tiles // 2):
+            at = 2 * q * row_tile
+            pair = [picked[:, at : at + row_tile], picked[:, at + row_tile : at + 2 * row_tile]]
+            rows[t, af * (tiles // 2) + q] = jnp.concatenate(pair, axis=0).astype(bf16)
+        for off in range(1, n_af):
+            row_message(t, off).start()
+
+    waiting = None
     for t in range(STEPS):
         first, last = t, planes - 2 - t
+        end = t + 1 == STEPS
         for c in range(2):
             along_z(ef, c, first, last - first + 1, ahead, wide)
         for p in range(first, last + 1):
@@ -354,16 +425,22 @@
                     (ef[1, p + 1, y] - ey[y]) - (ex_y[y] - ex[y]),
                 )
                 mask = low_mask[(2 if p < halo else 0) + y]
-                for c in range(3):
-                    new = change[c] * mask
+                if end and y:
+                    needed, w = (0, 2), slice(0, cz)
+                else:
+                    needed, w = (0, 1, 2), slice(0, wide)
+                for c in needed:
+                    new = change[c][:, w] * mask[:, w]
                     if t:
-                        new = gf[c, p, y] + new
-                    gf[c, p, y] = new
+                        new = gf[c, p, y, :, w] + new
+                    gf[c, p, y, :, w] = new
+        magnetic_rows = pick(None, gf)
+        if waiting is not None:
+            send_rows(*waiting)
         first = t + 1
-        end = t + 1 == STEPS
         width = cz if end else wide
         for c in range(2):
-            along_z(gf, c, first, last - first + 1, behind, width)
+            along_z(gf, c, first, last - first + 1, behind, width, 1 if end else 2)
         for p in range(first, last + 1):
             hx, hz = [[gf[c, p, y] for y in range(2)] for c in (0, 2)]
             hx_y, hz_y = down_y(hx), down_y(hz)
@@ -381,51 +458,34 @@
                         h_out[c, p - halo] = -COURANT * gf[c, p, 0, :, w]
                     else:
                         ef[c, p, y] = new
-        if end:
-            stores[0].start()
-            stores[1].start()
-
-        picked = []
-        for k in range(comps):
-            if end:
-                field = (e_out if k < 3 else h_out)[k % 3]
-            else:
-                field = (ef if k < 3 else gf)[k % 3, halo : halo + cx, 0, :, 0:cz]
-            values = field.reshape(cx * cy, cz)
-            if k >= 3 and not end:
-                values = -COURANT * values
-            column = jnp.dot(values.astype(bf16), zhot[...], preferred_element_type=f32)
-            picked.append(jnp.sum(column * rhot[...], axis=0, keepdims=True))
-        picked.append(jnp.zeros((8 - comps, hmax), jnp.float32))
-        picked = jnp.concatenate(picked, axis=0)
-        for q in range(tiles // 2):
-            at = 2 * q * row_tile
-            pair = [picked[:, at : at + row_tile], picked[:, at + row_tile : at + 2 * row_tile]]
-            rows[t, af * (tiles // 2) + q] = jnp.concatenate(pair, axis=0).astype(jnp.bfloat16)
-        for off in range(1, n_af):
-            row_message(t, off).start()
+        electric_rows = pick(e_out if end else None, ef)
+        if not end:
+            waiting = (t, electric_rows, magnetic_rows)
+    send_rows(STEPS - 1, electric_rows, magnetic_rows)
+    stores[0].start()
+    stores[1].start()
 
     loads[-1].wait()
+
     for t in range(STEPS):
         for off in range(1, n_af):
             row_message(t, off).wait_recv()
-
     sums = []
     for o in range(owned):
-        total = None
+        segments, blocks = [], []
         for n in range(entries):
             tile = band[0, o, n]
-            pairs = [rows[t, tile // 2].astype(jnp.float32) for t in range(STEPS)]
+            pairs = [rows[t, tile // 2].astype(f32) for t in range(STEPS)]
             odd = lax.rem(tile, 2)
-            segment = jnp.concatenate(
-                [jnp.where(odd == 1, pair[8:], pair[:8]) for pair in pairs], axis=0)
-            term = lax.dot_general(
-                segment.astype(jnp.bfloat16),
-                weights[o, 0, n].reshape(comps * row_tile, row_tile),
-                (((1,), (1,)), ((), ())),
-                preferred_element_type=jnp.float32,
-            )
-            total = term if total is None else total + term
+            segments.append(jnp.concatenate(
+                [jnp.where(odd == 1, pair[8:], pair[:8]) for pair in pairs], axis=0))
+            blocks.append(weights[o, 0, n].reshape(comps * row_tile, row_tile))
+        total = lax.dot_general(
+            jnp.concatenate(segments, axis=1).astype(bf16),
+            jnp.concatenate(blocks, axis=1),
+            (((1,), (1,)), ((), ())),
+            preferred_element_type=f32,
+        )
         for t in range(STEPS):
             own = total[t * 8 : t * 8 + 1, 0:row_tile]
             for k in range(1, comps):
@@ -444,20 +504,18 @@
     for t in range(STEPS):
         for off in range(1, n_af):
             row_message(t, off).wait_send()
-    for step in STEPS_TO:
-        @pl.when(exists(step))
-        def _(step=step):
-            message(step).wait_send()
+    for m in range(len(MESSAGES)):
+        @pl.when(exists(MESSAGES[m][0]))
+        def _(m=m):
+            message(m).wait_send()
     stores[0].wait()
     stores[1].wait()
     over_groups(lambda off: share_message(off).wait_recv())
     total = jnp.sum(shares[...], axis=0)
     for o in range(owned):
         pattern[:, o * row_tile : (o + 1) * row_tile] = total[o * STEPS : (o + 1) * STEPS]
-    stores[2].start()
 
     over_groups(lambda off: share_message(off).wait_send())
-    stores[2].wait()
 
 
 def finish(e_in, h_in, p_in, e_out, h_out, p_out, sem):
@@ -495,11 +553,10 @@
         functools.partial(kernel, sizes),
         out_shape=out_shape,
         in_specs=[hbm] * 8,
-        out_specs=(anyw,) * 3,
+        out_specs=(anyw, anyw, pl.BlockSpec(memory_space=pltpu.VMEM)),
         scratch_shapes=[
             pltpu.VMEM(electric.shape, f32),
             pltpu.VMEM(electric.shape, f32),
-            pltpu.VMEM((STEPS, owned * row_tile), f32),
             pltpu.VMEM(material.shape, jnp.int32),
             pltpu.VMEM(coef_keep.shape, f32),
             pltpu.VMEM(coef_curl.shape, f32),
@@ -518,23 +575,25 @@
             pltpu.VMEM((2, 4, STEPS // 2, 2 * cy, cz), bf16),
             pltpu.VMEM((2, 4, cx // 4, 2 * cy, cz), bf16),
             pltpu.VMEM((2, 2 * cy, cz), bf16),
+            pltpu.VMEM((2, 2 * cy, cz), bf16),
             pltpu.VMEM((2, 4, STEPS // 2, 2 * cy, cz), bf16),
             pltpu.VMEM((2, 4, planes // 4, 2 * cy, cz), bf16),
-            pltpu.VMEM((2, 3, 3, 2, 2 * cy, cz), bf16),
+            pltpu.VMEM((2, 3, 2, 2 * cy, cz), bf16),
+            pltpu.VMEM((2, 2, 3, 2 * cy, cz), bf16),
             pltpu.VMEM((8, cz), f32),
-            pltpu.VMEM((cz, hmax), jnp.bfloat16),
-            pltpu.VMEM((cx * cy, hmax), f32),
+            pltpu.VMEM((4 * cz, hmax), bf16),
+            pltpu.VMEM((cx * cy // 4, hmax), f32),
             pltpu.VMEM((STEPS, tiles // 2, 16, row_tile), jnp.bfloat16),
             pltpu.VMEM(radiation.shape, jnp.bfloat16),
             pltpu.VMEM((groups, owned * STEPS, row_tile), f32),
-            pltpu.SemaphoreType.DMA((len(STEPS_TO),)),
-            pltpu.SemaphoreType.DMA((len(STEPS_TO),)),
+            pltpu.SemaphoreType.DMA((len(MESSAGES),)),
+            pltpu.SemaphoreType.DMA((len(MESSAGES),)),
             pltpu.SemaphoreType.DMA((STEPS, n_af)),
             pltpu.SemaphoreType.DMA((STEPS, n_af)),
             pltpu.SemaphoreType.DMA((groups,)),
             pltpu.SemaphoreType.DMA((groups,)),
             pltpu.SemaphoreType.DMA((8,)),
-            pltpu.SemaphoreType.DMA((3,)),
+            pltpu.SemaphoreType.DMA((2,)),
         ],
         compiler_params=pltpu.CompilerParams(
             collective_id=0, has_side_effects=True, vmem_limit_bytes=24 * 1024 * 1024

time: 26.2 us -> 24.5 us (0.935)
  Pallas kernels: 24.8 us -> 23.1 us
    pallas_call x1, Pallas kernels: 24 us -> 22.3 us  [on_device(): pl.pallas_call(functools.partial(kernel, sizes), out_shape=out_shape, in_...]
where the time goes in v3:
time: 24.5 us; the launch traced here: 24.4 us
  Pallas kernels  23.1 us (94%)
  between operations  1.29 us (5%)
    pallas_call x1, Pallas kernels, on_device(): pl.pallas_call(functools.partial(kernel, sizes), out_shape=out_shape, in_...  22.3 us
    pallas_call x1, Pallas kernels, on_device(): pl.pallas_call(finish, out_shape=out_shape, in_specs=[anyw] * 3, out_spec...  0.77 us

profile of v3, /device:TPU:0, one launch (start us, length us, event | category | flops | bytes accessed | tf_op | source)
XLA Modules:
  0.0 24.4 jit_solution(13466696269841894893)
XLA Ops:
  1.3 22.3 %shard_map.103 = (f32[3,16,8,128]{3,2,1,0:T(8,128)S(1)}, f32[3,16,8,128]{3,2,1,0:T(8,128)S(1)}, f32[4,256]{1,0:T(4,128)S(1)}) custom-call(f32[3,16,8,128]{3,2,1,0:T(8,128)} %electric_in.1, s32[16,8,128]{2,1,0:T(8,128)} %material_in.1, f32[3,16]{1,0:T(4,128)} %keep_in.1, f32[3,16]{1,0:T(4,128)} %curl_in.1, s32[1,1,1]{2,1,0:T(1,128)S(6)} %copy.11.count_in, ...), custom_call_target="tpu_custom_call" | custom-call | tf_op jit(solution)/shard_map/pallas_call | solution.py:552
  23.6 0.8 %shard_map.104 = (f32[3,16,8,128]{3,2,1,0:T(8,128)}, f32[3,16,8,128]{3,2,1,0:T(8,128)}, f32[4,256]{1,0:T(4,128)}) custom-call(f32[3,16,8,128]{3,2,1,0:T(8,128)S(1)} %get-tuple-element.6.e_in, f32[3,16,8,128]{3,2,1,0:T(8,128)S(1)} %get-tuple-element.7.h_in, f32[4,256]{1,0:T(4,128)S(1)} %get-tuple-element.8.p_in), custom_call_target="tpu_custom_call" | custom-call | tf_op jit(solution)/shard_map/pallas_call | solution.py:602

commit v4 on v3

--- a/solution.py
+++ b/solution.py
@@ -10,6 +10,7 @@
 
 STEPS = 4
 COURANT = 0.5
+TURNED = 8
 MESH = pl.DeviceIdType.MESH
 f32, bf16 = jnp.float32, jnp.bfloat16
 
@@ -300,6 +301,13 @@
                     else:
                         set_factors(p, 0, as_classes(v))
 
+    receive(lambda d, part: d[1] and not d[2] and not part)
+    for c in range(3):
+        def put(p, v, c=c):
+            ef[c, p, 1, :, 0:cz] = v
+
+        beside_y(c, put)
+
     receive(lambda d, part: d[2])
     from_above = lax.rem(lane, edge) < halo
 
@@ -350,13 +358,6 @@
                         at_row += 6 * cy
                         gain[c, p, t, :, cz:wide] = b[at_row : at_row + cy, cols]
 
-    receive(lambda d, part: d[1] and not d[2] and not part)
-    for c in range(3):
-        def put(p, v, c=c):
-            ef[c, p, 1, :, 0:cz] = v
-
-        beside_y(c, put)
-
     def row_message(t, off):
         mine = rows.at[t, pl.ds(af * (tiles // 2), tiles // 2)]
         return pltpu.make_async_remote_copy(
@@ -414,14 +415,18 @@
         first, last = t, planes - 2 - t
         end = t + 1 == STEPS
         for c in range(2):
-            along_z(ef, c, first, last - first + 1, ahead, wide)
+            along_z(ef, c, first, last - first + 1 - TURNED, ahead, wide)
         for p in range(first, last + 1):
             ex, ey, ez = [[ef[c, p, y] for y in range(2)] for c in range(3)]
             ez_y, ex_y = up_y(ez), up_y(ex)
             for y in range(2):
+                if p > last - TURNED:
+                    z_x, z_y = [pltpu.roll(v[y], wide - 1, 1) - v[y] for v in (ex, ey)]
+                else:
+                    z_x, z_y = dz[0, p, y], dz[1, p, y]
                 change = (
-                    (ez_y[y] - ez[y]) - dz[1, p, y],
-                    dz[0, p, y] - (ef[2, p + 1, y] - ez[y]),
+                    (ez_y[y] - ez[y]) - z_y,
+                    z_x - (ef[2, p + 1, y] - ez[y]),
                     (ef[1, p + 1, y] - ey[y]) - (ex_y[y] - ex[y]),
                 )
                 mask = low_mask[(2 if p < halo else 0) + y]
@@ -440,15 +445,20 @@
         first = t + 1
         width = cz if end else wide
         for c in range(2):
-            along_z(gf, c, first, last - first + 1, behind, width, 1 if end else 2)
+            along_z(gf, c, first, last - first + 1 - TURNED, behind, width, 1 if end else 2)
         for p in range(first, last + 1):
             hx, hz = [[gf[c, p, y] for y in range(2)] for c in (0, 2)]
             hx_y, hz_y = down_y(hx), down_y(hz)
             for y in range(1 if end else 2):
                 w = slice(0, width)
+                if p > last - TURNED:
+                    z_x, z_y = [
+                        (v - pltpu.roll(v, 1, 1))[:, w] for v in (hx[y], gf[1, p, y])]
+                else:
+                    z_x, z_y = dz[0, p, y, :, w], dz[1, p, y, :, w]
                 change = (
-                    (hz[y] - hz_y[y])[:, w] - dz[1, p, y, :, w],
-                    dz[0, p, y, :, w] - (hz[y] - gf[2, p - 1, y])[:, w],
+                    (hz[y] - hz_y[y])[:, w] - z_y,
+                    z_x - (hz[y] - gf[2, p - 1, y])[:, w],
                     (gf[1, p, y] - gf[1, p - 1, y])[:, w] - (hx[y] - hx_y[y])[:, w],
                 )
                 for c in range(3):

time: 24.5 us -> 24.1 us (0.984)
  Pallas kernels: 23.1 us -> 22.6 us
    pallas_call x1, Pallas kernels: 22.3 us -> 21.9 us  [on_device(): pl.pallas_call(functools.partial(kernel, sizes), out_shape=out_shape, in_...]
where the time goes in v4:
time: 24.1 us; the launch traced here: 23.9 us
  Pallas kernels  22.6 us (94%)
  between operations  1.29 us (5%)
    pallas_call x1, Pallas kernels, on_device(): pl.pallas_call(functools.partial(kernel, sizes), out_shape=out_shape, in_...  21.9 us
    pallas_call x1, Pallas kernels, on_device(): pl.pallas_call(finish, out_shape=out_shape, in_specs=[anyw] * 3, out_spec...  0.77 us

profile of v4, /device:TPU:0, one launch (start us, length us, event | category | flops | bytes accessed | tf_op | source)
XLA Modules:
  0.0 23.9 jit_solution(1101327582139754507)
XLA Ops:
  1.3 21.9 %shard_map.103 = (f32[3,16,8,128]{3,2,1,0:T(8,128)S(1)}, f32[3,16,8,128]{3,2,1,0:T(8,128)S(1)}, f32[4,256]{1,0:T(4,128)S(1)}) custom-call(f32[3,16,8,128]{3,2,1,0:T(8,128)} %electric_in.1, s32[16,8,128]{2,1,0:T(8,128)} %material_in.1, f32[3,16]{1,0:T(4,128)} %keep_in.1, f32[3,16]{1,0:T(4,128)} %curl_in.1, s32[1,1,1]{2,1,0:T(1,128)S(6)} %copy.11.count_in, ...), custom_call_target="tpu_custom_call" | custom-call | tf_op jit(solution)/shard_map/pallas_call | solution.py:562
  23.2 0.8 %shard_map.104 = (f32[3,16,8,128]{3,2,1,0:T(8,128)}, f32[3,16,8,128]{3,2,1,0:T(8,128)}, f32[4,256]{1,0:T(4,128)}) custom-call(f32[3,16,8,128]{3,2,1,0:T(8,128)S(1)} %get-tuple-element.6.e_in, f32[3,16,8,128]{3,2,1,0:T(8,128)S(1)} %get-tuple-element.7.h_in, f32[4,256]{1,0:T(4,128)S(1)} %get-tuple-element.8.p_in), custom_call_target="tpu_custom_call" | custom-call | tf_op jit(solution)/shard_map/pallas_call | solution.py:612
